TPU v7x, 512 devices: a whole 4x4x16 slice. The times are simulated.
512 devices in a mesh: rows: 64 (over z, x_hi, core), feat: 8 (over y, x_lo).
Axes of the slice: x: 4 (x_hi: 2, x_lo: 2; x = x_hi * 2 + x_lo), y: 4, z: 16, core: 2. Of those that a mesh axis runs over, the one named last changes fastest.
Arguments:
- gradients: bfloat16 [65536, 8192], P('rows', 'feat'), may hold values from -2500 to 2500
- queries: bfloat16 [1024, 8192], P('rows', 'feat'), may hold values from -0.1875 to 0.1875
- loss_weight: float32 [65536], P('rows'), may hold values from 0.09 to 1
Outputs:
- standardized: bfloat16 [65536, 1024], P('rows', 'feat')
All inputs are finite; a program needn't handle non-finite values.
Results may differ from a plain program's by a relative error of at most 0.019.
Values may be sent and summed in bfloat16 or wider, within the bound.
A program may use at most 64 MiB of HBM per device.

v0:
```python
import jax
import jax.numpy as jnp
from jax import lax
from jax.sharding import PartitionSpec as P

NORM_EPS = 1e-06
VAR_EPS = 1e-05


def body(gradients, queries, loss_weight):
    rows_here = gradients.shape[0]
    total_rows = rows_here * lax.axis_size("rows")
    feature_count = gradients.shape[1] * lax.axis_size("feat")
    local_squares = jnp.sum(jnp.square(gradients.astype(jnp.float32)), axis=1)
    squares = lax.psum(local_squares, "feat")
    product = lax.dot_general(
        gradients,
        lax.all_gather(queries, "rows", axis=0, tiled=True),
        (((1,), (1,)), ((), ())),
        preferred_element_type=jnp.float32,
    )
    partial_value = product.astype(jnp.bfloat16)
    partial_float = partial_value.astype(jnp.float32)
    query_share = partial_value.shape[1] // lax.axis_size("feat")
    summed = lax.psum(partial_float.astype(jnp.bfloat16), "feat").astype(jnp.float32)
    raw = lax.dynamic_slice_in_dim(summed, lax.axis_index("feat") * query_share, query_share, 1)
    factor = loss_weight / jnp.sqrt(squares / feature_count + NORM_EPS)
    scored = raw * factor[:, None]
    sums = lax.psum(jnp.sum(scored, axis=0), "rows")
    column_mean = sums / total_rows
    centered = scored - column_mean[None, :]
    square_sums = lax.psum(jnp.sum(centered * centered, axis=0), "rows")
    column_var = square_sums / total_rows
    return (centered * lax.rsqrt(column_var + VAR_EPS)[None, :]).astype(jnp.bfloat16)


def solution(mesh):
    in_specs = (P("rows", "feat"), P("rows", "feat"), P("rows"))
    out_specs = P("rows", "feat")
    return jax.shard_map(body, mesh=mesh, in_specs=in_specs, out_specs=out_specs, check_vma=False)
```

profile of v0, /device:TPU:1, one launch (start us, length us, event | category | flops | bytes accessed | tf_op | source)
XLA Modules:
  0.0 554.2 jit_solution(9784437294390381121)
XLA Ops:
  6.5 0.0 all-gather.2.cloned.1.call-start
  6.5 0.7 all-gather.2.cloned.1.call-update
  7.3 0.0 all-reduce.2.cloned.1.call-start
  7.3 152.9 %all-gather.2.cloned.1.call-done = bf16[1024,1024]{1,0:T(8,128)(2,1)} async-done(((bf16[16,1024]{1,0:T(8,128)(2,1)}), bf16[1024,1024]{1,0:T(8,128)(2,1)}) %all-gather.2.cloned.1.call-update) | async-done | bytes 2097168 | tf_op jit(solution)/shard_map/all_gather | solution.py:18
  160.2 5.9 %convolution_convert_fusion = bf16[1024,1024]{1,0:T(8,128)(2,1)} fusion(bf16[1024,1024]{1,0:T(8,128)(2,1)} %param.3, bf16[1024,1024]{1,0:T(8,128)(2,1)} %all-gather.2.cloned.1.call-done), kind=kOutput, calls=%fused_computation.1 | convolution fusion | flops 2148532224 | bytes 6291456 | tf_op jit(solution)/shard_map/dot_general | solution.py:16
  166.1 0.0 copy-start
  166.1 0.0 copy-start.1
  166.1 0.0 all-reduce.2.cloned.1.call-update
  166.2 1.6 copy-done
  167.7 0.5 multiply_reduce_fusion
  168.2 15.4 %psum.29 = f32[1024]{0:T(1024)S(1)} all-reduce(f32[1024]{0:T(1024)S(1)} %multiply_reduce_fusion), channel_id=1, replica_groups=mesh['rows'=64,'feat'=8] {'feat'}, use_global_device_ids=true, to_apply=%region_2.0 | all-reduce | flops 1024 | bytes 8192 | tf_op jit(solution)/shard_map/psum | solution.py:15
  183.6 0.0 copy-done.1
  183.6 96.5 %all-reduce.2.cloned.1.call-done = bf16[1024,1024]{1,0:T(8,128)(2,1)} async-done(((bf16[1024,1024]{1,0:T(8,128)(2,1)}), bf16[1024,1024]{1,0:T(8,128)(2,1)}) %all-reduce.2.cloned.1.call-update) | async-done | bytes 2097168 | tf_op jit(solution)/shard_map/psum | solution.py:25
  280.1 1.2 fusion.1
  281.2 129.9 %psum.30 = f32[128]{0:T(128)S(1)} all-reduce(f32[128]{0:T(128)S(1)} %fusion.1), channel_id=1, replica_groups=mesh['rows'=64,'feat'=8] {'rows'}, use_global_device_ids=true, to_apply=%region_4.0 | all-reduce | flops 128 | bytes 1024 | tf_op jit(solution)/shard_map/psum | solution.py:29
  411.2 1.2 multiply_reduce_fusion.1
  412.3 133.2 %psum.31 = f32[128]{0:T(128)S(1)} all-reduce(f32[128]{0:T(128)S(1)} %multiply_reduce_fusion.1), channel_id=1, replica_groups=mesh['rows'=64,'feat'=8] {'rows'}, use_global_device_ids=true, to_apply=%region_6.0 | all-reduce | flops 128 | bytes 1024 | tf_op jit(solution)/shard_map/psum | solution.py:32
  545.5 1.9 multiply_convert_fusion
  (3 shorter events, 0.0 us)
Async XLA Ops:
  6.5 153.6 %all-gather.2.cloned.1.call-start = ((), (), s32[]{:S(2)}) async-start(), calls=%async_computation | async-start | bytes 2129920 | tf_op jit(solution)/shard_map/all_gather | solution.py:18
  7.3 272.8 %all-reduce.2.cloned.1.call-start = ((), (), s32[]{:S(2)}) async-start(), calls=%async_computation.1 | async-start | bytes 4194304 | tf_op jit(solution)/shard_map/psum | solution.py:25
  166.1 1.6 copy-start
  166.1 17.4 %copy-start.1 = (f32[1024]{0:T(1024)S(1)}, f32[1024]{0:T(1024)}, u32[]{:S(2)}) copy-start(f32[1024]{0:T(1024)} %param.5) | copy-start | bytes 12292
Sparse Core Ops, SparseCore 0:
  10.6 149.4 all-gather.1
  166.3 113.7 all-reduce.1
where the time goes:
time: 555 us; the launch traced here: 554 us
  blocking collectives  278 us (50%)
  waiting for transfers between devices  250 us (45%)
  between operations  13.4 us (2%)
  matrix products  5.94 us (1%)
    all_gather x1, waiting for transfers between devices, body(): lax.all_gather(queries, 'rows', axis=0, tiled=True)  153 us
    psum x1, blocking collectives, body(): square_sums = lax.psum(jnp.sum(centered * centered, axis=0), 'rows')  133 us
    psum x1, blocking collectives, body(): sums = lax.psum(jnp.sum(scored, axis=0), 'rows')  130 us
    psum x1, waiting for transfers between devices, body(): lax.psum(partial_float.astype(jnp.bfloat16), 'feat').astype(jnp.float32)  96.5 us
    psum x1, blocking collectives, body(): squares = lax.psum(local_squares, 'feat')  15.4 us
  transfers between devices with their start and end apart: 2, of which 2 were waited for; matrix products, arithmetic and copies ran while one was open for 0% of the time, Pallas kernels for 0%

commit v1 on v0

v1 whole, which is shorter than its diff:
```python
import functools
import jax
import jax.numpy as jnp
from jax import lax
from jax.experimental import pallas as pl
from jax.experimental.pallas import tpu as pltpu
from jax.sharding import PartitionSpec as P

NORM_EPS = 1e-06
VAR_EPS = 1e-05

NZ, NR, NF = 16, 64, 8
QB = 16
CHUNKS = 4
MESH = pl.DeviceIdType.MESH

FIRST, SECOND = (3, -3, 1, -1), (6, -6)
THIRD, LAST = (4, -4, 2, -2), (7, -7, 5, -5, 8)


def kernel(
    g_ref, q_ref, lw_ref, o_ref,
    qall, part, got, sq_mine, sq_got, scored, fac, stat_mine, stat_got,
    z_send, z_recv, x_send, x_recv, c_send, c_recv, d_send, d_recv,
    f_send, f_recv, s_send, s_recv, t_send, t_recv,
):
    r, f = lax.axis_index("rows"), lax.axis_index("feat")
    z, xh, c = r // 4, lax.rem(r // 2, 2), lax.rem(r, 2)
    rows = g_ref.shape[0]
    cols = g_ref.shape[1]

    def at(dz, xh_to, c_to):
        return (lax.rem(z + dz + NZ, NZ) * 4 + xh_to * 2 + c_to, f)

    def block(dz, xh_of, c_of):
        first = (lax.rem(z + dz + NZ, NZ) * 4 + xh_of * 2 + c_of) * QB
        return qall.at[pl.ds(pl.multiple_of(first, QB), QB)]

    def feat_peer(k):
        return (r, lax.rem(f + k, NF))

    barrier = pltpu.get_barrier_semaphore()
    greet = [at(d, xh, c) for d in (1, -1, 3, -3, 4 * c - 2)]
    greet += [at(0, 1 - xh, c), at(0, xh, 1 - c)]
    greet += [feat_peer(k) for k in range(1, NF)]
    for device in greet:
        pl.semaphore_signal(barrier, inc=1, device_id=device, device_id_type=MESH)

    lanes = 128
    for i in range(8):
        piece = rows // 8
        sums = jnp.zeros((piece, lanes), jnp.float32)
        for j in range(cols // lanes):
            v = g_ref[i * piece:(i + 1) * piece, j * lanes:(j + 1) * lanes].astype(jnp.float32)
            sums = sums + v * v
        sq_mine[:, i * piece:(i + 1) * piece] = jnp.sum(jnp.transpose(sums), axis=0, keepdims=True)
    block(0, xh, c)[...] = q_ref[...]

    pl.semaphore_wait(barrier, len(greet))

    sends = []

    def push(src, dst, ssem, rsem, device):
        copy = pltpu.make_async_remote_copy(
            src_ref=src, dst_ref=dst, send_sem=ssem, recv_sem=rsem,
            device_id=device, device_id_type=MESH)
        copy.start()
        sends.append(copy)

    def landed(dst, rsem):
        pltpu.make_async_remote_copy(
            src_ref=dst, dst_ref=dst, send_sem=z_send.at[0], recv_sem=rsem,
            device_id=at(0, xh, 1 - c), device_id_type=MESH).wait_recv()

    count = [0]

    def z_push(d, step):
        here = block(-d, xh, c)
        push(here, here, z_send.at[count[0]], z_recv.at[(d + step) % NZ], at(step, xh, c))
        count[0] += 1

    def share(d):
        here = block(-d, xh, c)
        push(here, here, x_send.at[d % NZ], x_recv.at[d % NZ], at(0, 1 - xh, c))
        push(here, here, c_send.at[d % NZ], c_recv.at[d % NZ], at(0, xh, 1 - c))

    def share_x(d):
        here = block(-d, 1 - xh, c)
        landed(here, x_recv.at[d % NZ])
        push(here, here, d_send.at[d % NZ], d_recv.at[d % NZ], at(0, xh, 1 - c))

    for step in (3, -3, 1, -1):
        z_push(0, step)
    share(0)
    for k in range(1, NF):
        push(sq_mine, sq_got.at[k - 1], s_send.at[k - 1], s_recv.at[k - 1], feat_peer(k))
    for d in FIRST:
        landed(block(-d, xh, c), z_recv.at[d % NZ])
        if d == 3:
            for step in (3, 1, -1):
                z_push(d, step)
        if d == -3:
            for step in (-3, -1, 1):
                z_push(d, step)
        share(d)
    share_x(0)
    for d in SECOND:
        landed(block(-d, xh, c), z_recv.at[d % NZ])
        z_push(d, 1)
        z_push(d, -1)
        if d == -6:
            turn = 1 - 2 * c
            here = block(-6 * turn, xh, c)
            push(here, here, z_send.at[count[0]], z_recv.at[8], at(2 * turn, xh, c))
            count[0] += 1
        share(d)
    for d in THIRD:
        landed(block(-d, xh, c), z_recv.at[d % NZ])
        share(d)
    for d in FIRST:
        share_x(d)

    total = sq_mine[...]
    for k in range(1, NF):
        landed(sq_got.at[k - 1], s_recv.at[k - 1])
        total = total + sq_got[k - 1]
    factor = lw_ref[...] / jnp.sqrt(total / (cols * NF) + NORM_EPS)
    fac[...] = jnp.transpose(jnp.broadcast_to(factor, (lanes, rows)))

    for d in LAST:
        landed(block(-d, xh, c), z_recv.at[d % NZ])
        share(d)
    for d in SECOND + THIRD + LAST:
        share_x(d)
    for d in (0,) + FIRST + SECOND + THIRD + LAST:
        landed(block(-d, xh, 1 - c), c_recv.at[d % NZ])
        landed(block(-d, 1 - xh, 1 - c), d_recv.at[d % NZ])

    size = rows // CHUNKS
    share_w = o_ref.shape[1]

    def chunk_copy(i, k):
        span = pl.ds(pl.multiple_of(i * size, size), size)
        to = lax.rem(f + k, NF)
        return pltpu.make_async_remote_copy(
            src_ref=part.at[to, span], dst_ref=got.at[k - 1, span],
            send_sem=f_send.at[i, k - 1], recv_sem=f_recv.at[i, k - 1],
            device_id=(r, to), device_id_type=MESH)

    @pl.loop(0, CHUNKS)
    def _(i):
        span = pl.ds(pl.multiple_of(i * size, size), size)
        product = lax.dot_general(g_ref[span, :], qall[...], (((1,), (1,)), ((), ())),
                                  preferred_element_type=jnp.float32)
        for b in range(NF):
            part[b, span, :] = product[:, b * share_w:(b + 1) * share_w].astype(jnp.bfloat16)
        for k in range(1, NF):
            chunk_copy(i, k).start()

    def take(i, column_sum):
        span = pl.ds(pl.multiple_of(i * size, size), size)
        raw = part[f, span, :].astype(jnp.float32)
        for k in range(1, NF):
            chunk_copy(i, k).wait_recv()
            raw = raw + got[k - 1, span, :].astype(jnp.float32)
        value = raw * fac[span, :]
        scored[span, :] = value
        return column_sum + jnp.sum(value, axis=0, keepdims=True)

    column_sum = lax.fori_loop(0, CHUNKS, take, jnp.zeros((1, share_w), jnp.float32))
    own_mean = column_sum / rows
    off = scored[...] - own_mean
    stat_mine[0:1, :] = own_mean
    stat_mine[1:2, :] = jnp.sum(off * off, axis=0, keepdims=True)

    def stat_copy(i):
        return pltpu.make_async_remote_copy(
            src_ref=stat_mine, dst_ref=stat_got.at[i - 1],
            send_sem=t_send.at[i - 1], recv_sem=t_recv.at[i - 1],
            device_id=(lax.rem(r + i, NR), f), device_id_type=MESH)

    @pl.loop(1, NR)
    def _(i):
        stat_copy(i).start()

    @pl.loop(1, NR)
    def _(i):
        stat_copy(i).wait_recv()

    means = stat_got[:, 0, :]
    mean = (jnp.sum(means, axis=0, keepdims=True) + own_mean) / NR
    apart = means - mean
    own_apart = own_mean - mean
    spread = jnp.sum(stat_got[:, 1, :], axis=0, keepdims=True) + stat_mine[1:2, :]
    spread = spread + rows * (jnp.sum(apart * apart, axis=0, keepdims=True) + own_apart * own_apart)
    scale = lax.rsqrt(spread / (rows * NR) + VAR_EPS)
    o_ref[...] = ((scored[...] - mean) * scale).astype(o_ref.dtype)

    for copy in sends:
        copy.wait_send()

    @pl.loop(0, CHUNKS)
    def _(i):
        for k in range(1, NF):
            chunk_copy(i, k).wait_send()

    @pl.loop(1, NR)
    def _(i):
        stat_copy(i).wait_send()


def body(gradients, queries, loss_weight):
    rows, cols = gradients.shape
    width = queries.shape[0] * NR // NF
    dma = pltpu.SemaphoreType.DMA
    return pl.pallas_call(
        kernel,
        out_shape=jax.ShapeDtypeStruct((rows, width), jnp.bfloat16),
        in_specs=[pl.BlockSpec(memory_space=pltpu.VMEM)] * 3,
        out_specs=pl.BlockSpec(memory_space=pltpu.VMEM),
        scratch_shapes=[
            pltpu.VMEM((NR * QB, cols), jnp.bfloat16),
            pltpu.VMEM((NF, rows, width), jnp.bfloat16),
            pltpu.VMEM((NF - 1, rows, width), jnp.bfloat16),
            pltpu.VMEM((1, rows), jnp.float32),
            pltpu.VMEM((NF - 1, 1, rows), jnp.float32),
            pltpu.VMEM((rows, width), jnp.float32),
            pltpu.VMEM((rows, width), jnp.float32),
            pltpu.VMEM((2, width), jnp.float32),
            pltpu.VMEM((NR - 1, 2, width), jnp.float32),
            dma((NZ - 1,)), dma((NZ,)), dma((NZ,)), dma((NZ,)),
            dma((NZ,)), dma((NZ,)), dma((NZ,)), dma((NZ,)),
            dma((CHUNKS, NF - 1)), dma((CHUNKS, NF - 1)),
            dma((NF - 1,)), dma((NF - 1,)), dma((NR - 1,)), dma((NR - 1,)),
        ],
        compiler_params=pltpu.CompilerParams(
            collective_id=0, has_side_effects=True, vmem_limit_bytes=40 * 2**20),
        cost_estimate=pl.CostEstimate(
            flops=2 * rows * NR * QB * cols, bytes_accessed=2 * rows * (cols + width), transcendentals=0),
        name="scores",
    )(gradients, queries, loss_weight.reshape(1, rows))


def solution(mesh):
    in_specs = (P("rows", "feat"), P("rows", "feat"), P("rows"))
    out_specs = P("rows", "feat")
    return jax.shard_map(body, mesh=mesh, in_specs=in_specs, out_specs=out_specs, check_vma=False)
```

time: 555 us -> 77.7 us (0.14)
  blocking collectives: 278 us -> 0 us
  waiting for transfers between devices: 250 us -> 0 us
  Pallas kernels: 0 us -> 73.7 us
  between operations: 13.4 us -> 0.01 us
  matrix products: 5.94 us -> 0 us
    psum x3 -> x0, blocking collectives: 278 us -> none  [the longest x1 133 us: body(): square_sums = lax.psum(jnp.sum(centered * centered, axis=0), 'rows')]
    all_gather x1 -> x0, waiting for transfers between devices: 153 us -> none  [body(): lax.all_gather(queries, 'rows', axis=0, tiled=True)]
    psum x1 -> x0, waiting for transfers between devices: 96.5 us -> none  [body(): lax.psum(partial_float.astype(jnp.bfloat16), 'feat').astype(jnp.float32)]
    pallas_call x0 -> x1, Pallas kernels: none -> 73.7 us  [body(): pl.pallas_call(kernel, out_shape=jax.ShapeDtypeStruct((rows, width), jnp....]
    dot_general x1 -> x0, matrix products: 5.94 us -> none  [body(): lax.dot_general(gradients, lax.all_gather(queries, 'rows', axis=0, tiled=...]
  transfers between devices with their start and end apart: 2 -> 0, of which waited for: 2 -> 0; matrix products, arithmetic and copies ran while one was open for 0% -> 0% of each run, Pallas kernels for 0% -> 0%
where the time goes in v1:
time: 77.7 us; the launch traced here: 77.5 us
  Pallas kernels  73.7 us (95%)
  local copies, waits for them, and re-layouts  3.74 us (5%)
    pallas_call x1, Pallas kernels, body(): pl.pallas_call(kernel, out_shape=jax.ShapeDtypeStruct((rows, width), jnp....  73.7 us
    unnamed x7, local copies, waits for them, and re-layouts  3.74 us

profile of v1, /device:TPU:1, one launch (start us, length us, event | category | flops | bytes accessed | tf_op | source)
XLA Modules:
  0.0 77.5 jit_solution(12739363673535982154)
XLA Ops:
  0.0 0.0 copy-start
  0.0 1.6 %copy-done = bf16[1024,1024]{1,0:T(8,128)(2,1)S(1)} copy-done((bf16[1024,1024]{1,0:T(8,128)(2,1)S(1)}, bf16[1024,1024]{1,0:T(8,128)(2,1)}, u32[]{:S(2)}) %copy-start) | copy-done | bytes 2097176
  1.6 0.0 copy-start.1
  1.6 0.8 copy-done.1
  2.4 0.0 copy-start.2
  2.4 0.7 copy-done.2
  3.0 73.7 %scores.1 = bf16[1024,128]{1,0:T(8,128)(2,1)S(1)} custom-call(bf16[1024,1024]{1,0:T(8,128)(2,1)S(1)} %copy-done, bf16[16,1024]{1,0:T(8,128)(2,1)S(1)} %copy-done.1, f32[1,1024]{1,0:T(1,128)S(1)} %bitcast.1), custom_call_target="tpu_custom_call" | custom-call | flops 2147483648 | bytes 2359296 | tf_op jit(solution)/shard_map/scores/pallas_call | solution.py:216
  76.8 0.7 copy.5
Async XLA Ops:
  0.0 1.6 %copy-start = (bf16[1024,1024]{1,0:T(8,128)(2,1)S(1)}, bf16[1024,1024]{1,0:T(8,128)(2,1)}, u32[]{:S(2)}) copy-start(bf16[1024,1024]{1,0:T(8,128)(2,1)} %g_ref.1) | copy-start | bytes 6291460
  1.6 0.8 copy-start.1
  2.4 0.7 copy-start.2

commit v2 on v1

v2 whole, which is shorter than its diff:
```python
import jax
import jax.numpy as jnp
from jax import lax
from jax.experimental import pallas as pl
from jax.experimental.pallas import tpu as pltpu
from jax.sharding import PartitionSpec as P

NORM_EPS = 1e-06
VAR_EPS = 1e-05

NZ, NR, NF, NY = 16, 64, 8, 4
QB = 16
CHUNKS = 4
LANES = 128
MESH = pl.DeviceIdType.MESH

FIRST, SECOND = (3, -3, 1, -1), (6, -6)
THIRD, LAST = (4, -4, 2, -2), (7, -7, 5, -5, 8)


def kernel(
    g_hbm, q_hbm, lw_hbm, o_ref,
    g, qall, lw, pa, pb, a_got, a_out, a_own, ax_got, bx_got, b_out, b_own, by_got,
    sq_mine, sq_got, sq_pair, sq_far, factor, scored, stat_mine, stat_got,
    l_sem, z_send, z_recv, x_send, x_recv, c_send, c_recv, d_send, d_recv,
    ay_send, ay_recv, ax_send, ax_recv, bx_send, bx_recv, by_send, by_recv,
    s_send, s_recv, t_send, t_recv,
):
    r, f = lax.axis_index("rows"), lax.axis_index("feat")
    z, xh, c = r // 4, lax.rem(r // 2, 2), lax.rem(r, 2)
    y, xl = f // 2, lax.rem(f, 2)
    rows, cols = g.shape
    size = rows // CHUNKS
    half = qall.shape[0] // 2
    per = half // NF

    def at(dz, xh_to, c_to):
        return (lax.rem(z + dz + NZ, NZ) * 4 + xh_to * 2 + c_to, f)

    def y_peer(k):
        return (r, lax.rem(y + k, NY) * 2 + xl)

    x_peer = (r, y * 2 + 1 - xl)

    def block(dz, xh_of, c_of):
        first = xh_of * half + lax.rem(z + dz + NZ, NZ) * (2 * QB) + c_of * QB
        return qall.at[pl.ds(pl.multiple_of(first, QB), QB)]

    loads = [
        pltpu.make_async_copy(q_hbm, block(0, xh, c), l_sem.at[0]),
        pltpu.make_async_copy(g_hbm, g, l_sem.at[1]),
        pltpu.make_async_copy(lw_hbm, lw, l_sem.at[2]),
    ]
    for load in loads:
        load.start()

    barrier = pltpu.get_barrier_semaphore()
    greet = [at(d, xh, c) for d in (3, -3, 4 * c - 2, 1, -1)]
    greet += [at(0, 1 - xh, c), at(0, xh, 1 - c), x_peer]
    greet += [y_peer(k) for k in range(1, NY)]
    for device in greet:
        pl.semaphore_signal(barrier, inc=1, device_id=device, device_id_type=MESH)
    loads[0].wait()
    pl.semaphore_wait(barrier, len(greet))

    sends = []

    def push(src, dst, ssem, rsem, device):
        copy = pltpu.make_async_remote_copy(
            src_ref=src, dst_ref=dst, send_sem=ssem, recv_sem=rsem,
            device_id=device, device_id_type=MESH)
        copy.start()
        sends.append(copy)

    def landed(dst, rsem):
        pltpu.make_async_remote_copy(
            src_ref=dst, dst_ref=dst, send_sem=z_send.at[0], recv_sem=rsem,
            device_id=at(0, xh, 1 - c), device_id_type=MESH).wait_recv()

    count = [0]

    def z_push(d, step):
        here = block(-d, xh, c)
        push(here, here, z_send.at[count[0]], z_recv.at[(d + step) % NZ], at(step, xh, c))
        count[0] += 1

    def share(d):
        here = block(-d, xh, c)
        push(here, here, x_send.at[d % NZ], x_recv.at[d % NZ], at(0, 1 - xh, c))
        push(here, here, c_send.at[d % NZ], c_recv.at[d % NZ], at(0, xh, 1 - c))

    def share_x(ds):
        for d in ds:
            here = block(-d, 1 - xh, c)
            landed(here, x_recv.at[d % NZ])
            push(here, here, d_send.at[d % NZ], d_recv.at[d % NZ], at(0, xh, 1 - c))

    for step in (3, -3, 1, -1):
        z_push(0, step)
    share(0)

    loads[1].wait()
    for i in range(rows // LANES):
        sums = jnp.zeros((LANES, LANES), jnp.float32)
        for j in range(cols // LANES):
            v = g[i * LANES:(i + 1) * LANES, j * LANES:(j + 1) * LANES].astype(jnp.float32)
            sums = sums + v * v
        sq_mine[:, i * LANES:(i + 1) * LANES] = jnp.sum(jnp.transpose(sums), axis=0, keepdims=True)
    for k in range(1, NY):
        push(sq_mine, sq_got.at[k - 1], s_send.at[k - 1], s_recv.at[k - 1], y_peer(k))

    for d in FIRST:
        landed(block(-d, xh, c), z_recv.at[d % NZ])
        if d == 3:
            for step in (3, 1, -1):
                z_push(d, step)
        if d == -3:
            for step in (-3, -1, 1):
                z_push(d, step)
        share(d)
    share_x((0,))
    for d in SECOND:
        landed(block(-d, xh, c), z_recv.at[d % NZ])
        z_push(d, 1)
        z_push(d, -1)
        if d == -6:
            turn = 1 - 2 * c
            here = block(-6 * turn, xh, c)
            push(here, here, z_send.at[count[0]], z_recv.at[8], at(2 * turn, xh, c))
            count[0] += 1
        share(d)
    share_x(FIRST[:2])
    for d in THIRD:
        landed(block(-d, xh, c), z_recv.at[d % NZ])
        share(d)

    total = sq_mine[...]
    for k in range(1, NY):
        landed(sq_got.at[k - 1], s_recv.at[k - 1])
        total = total + sq_got[k - 1]
    sq_pair[...] = total
    push(sq_pair, sq_far, s_send.at[NY - 1], s_recv.at[NY - 1], x_peer)
    share_x(FIRST[2:])

    for d in LAST:
        landed(block(-d, xh, c), z_recv.at[d % NZ])
        share(d)
    share_x(SECOND)
    for d in (0,) + FIRST + SECOND + THIRD + LAST:
        landed(block(-d, xh, 1 - c), c_recv.at[d % NZ])

    def product(xh_of, i):
        first = pl.multiple_of(xh_of * half, half)
        return lax.dot_general(
            qall[pl.ds(first, half), :], g[i * size:(i + 1) * size, :],
            (((1,), (1,)), ((), ())), preferred_element_type=jnp.float32)

    def multiply_a(i):
        value = product(xh, i)
        for b in range(NF):
            pa[i, b] = value[b * per:(b + 1) * per].astype(jnp.bfloat16)
        for k in (2, 1, 3):
            to = lax.rem(y + k, NY)
            push(pa.at[i, pl.ds(to * 2, 2)], a_got.at[i, k - 1],
                 ay_send.at[i, k - 1], ay_recv.at[i, k - 1], y_peer(k))

    def multiply_b(i):
        value = product(1 - xh, i)
        for b in range(NF):
            pb[i, b % 2, b // 2] = value[b * per:(b + 1) * per].astype(jnp.bfloat16)
        push(pb.at[i, 1 - xl], bx_got.at[i], bx_send.at[i], bx_recv.at[i], x_peer)

    def relay_a(i):
        near = pa[i, y * 2 + xl].astype(jnp.float32)
        far = pa[i, y * 2 + 1 - xl].astype(jnp.float32)
        for k in range(1, NY):
            landed(a_got.at[i, k - 1], ay_recv.at[i, k - 1])
            near = near + a_got[i, k - 1, xl].astype(jnp.float32)
            far = far + a_got[i, k - 1, 1 - xl].astype(jnp.float32)
        a_own[i] = near
        a_out[i] = far.astype(jnp.bfloat16)
        push(a_out.at[i], ax_got.at[i], ax_send.at[i], ax_recv.at[i], x_peer)

    def relay_b(i):
        landed(bx_got.at[i], bx_recv.at[i])
        for k in (2, 1, 3, 0):
            to = lax.rem(y + k, NY)
            both = pb[i, xl, to].astype(jnp.float32) + bx_got[i, to].astype(jnp.float32)
            if k == 0:
                b_own[i] = both
            else:
                b_out[i, k - 1] = both.astype(jnp.bfloat16)
                push(b_out.at[i, k - 1], by_got.at[i, k - 1],
                     by_send.at[i, k - 1], by_recv.at[i, k - 1], y_peer(k))

    for i, ds in enumerate((THIRD, LAST[:2], LAST[2:], ())):
        multiply_a(i)
        share_x(ds)
    for d in (0,) + FIRST + SECOND + THIRD + LAST:
        landed(block(-d, 1 - xh, 1 - c), d_recv.at[d % NZ])
    multiply_b(0)
    multiply_b(1)
    relay_a(0)
    multiply_b(2)
    multiply_b(3)

    landed(sq_far, s_recv.at[NY - 1])
    loads[2].wait()
    factor[...] = lw[...] / jnp.sqrt((sq_pair[...] + sq_far[...]) / (cols * NF) + NORM_EPS)

    relay_a(1)
    relay_b(0)
    relay_a(2)
    relay_b(1)
    relay_a(3)
    relay_b(2)
    relay_b(3)

    column_sum = jnp.zeros((1, LANES), jnp.float32)
    group = per // 2
    for i in range(CHUNKS):
        scale = factor[:, i * size:(i + 1) * size]
        landed(ax_got.at[i], ax_recv.at[i])
        own = (a_own[i] + ax_got[i].astype(jnp.float32)) * scale
        other = b_own[i]
        for k in range(1, NY):
            landed(by_got.at[i, k - 1], by_recv.at[i, k - 1])
            other = other + by_got[i, k - 1].astype(jnp.float32)
        other = other * scale
        low, high = jnp.where(xh == 0, own, other), jnp.where(xh == 0, other, own)
        value = jnp.transpose(jnp.concatenate(
            [low[:group], high[:group], low[group:], high[group:]], axis=0))
        scored[i * size:(i + 1) * size, :] = value
        column_sum = column_sum + jnp.sum(value, axis=0, keepdims=True)
    own_mean = column_sum / rows
    off = scored[...] - own_mean
    stat_mine[0:1, :] = own_mean
    stat_mine[1:2, :] = jnp.sum(off * off, axis=0, keepdims=True)

    def stat_copy(i):
        return pltpu.make_async_remote_copy(
            src_ref=stat_mine, dst_ref=stat_got.at[i - 1],
            send_sem=t_send.at[i - 1], recv_sem=t_recv.at[i - 1],
            device_id=(lax.rem(r + i, NR), f), device_id_type=MESH)

    far_first = sorted(range(1, NR), key=lambda i: abs(i - NR // 2))
    for i in far_first:
        stat_copy(i).start()

    @pl.loop(1, NR)
    def _(i):
        stat_copy(i).wait_recv()

    means = stat_got[:, 0, :]
    mean = (jnp.sum(means, axis=0, keepdims=True) + own_mean) / NR
    apart = means - mean
    own_apart = own_mean - mean
    spread = jnp.sum(stat_got[:, 1, :], axis=0, keepdims=True) + stat_mine[1:2, :]
    spread = spread + rows * (jnp.sum(apart * apart, axis=0, keepdims=True) + own_apart * own_apart)
    scale = lax.rsqrt(spread / (rows * NR) + VAR_EPS)
    o_ref[...] = ((scored[...] - mean) * scale).astype(o_ref.dtype)

    for copy in sends:
        copy.wait_send()

    @pl.loop(1, NR)
    def _(i):
        stat_copy(i).wait_send()


def body(gradients, queries, loss_weight):
    rows, cols = gradients.shape
    width = queries.shape[0] * NR // NF
    per, size = width // 2, rows // CHUNKS
    half, f32 = jnp.bfloat16, jnp.float32
    vmem, dma = pltpu.VMEM, pltpu.SemaphoreType.DMA
    return pl.pallas_call(
        kernel,
        out_shape=jax.ShapeDtypeStruct((rows, width), jnp.bfloat16),
        in_specs=[pl.BlockSpec(memory_space=pltpu.HBM)] * 3,
        out_specs=pl.BlockSpec(memory_space=pltpu.VMEM),
        scratch_shapes=[
            vmem((rows, cols), half),
            vmem((NR * QB, cols), half),
            vmem((1, rows), f32),
            vmem((CHUNKS, NF, per, size), half),
            vmem((CHUNKS, 2, NY, per, size), half),
            vmem((CHUNKS, NY - 1, 2, per, size), half),
            vmem((CHUNKS, per, size), half),
            vmem((CHUNKS, per, size), f32),
            vmem((CHUNKS, per, size), half),
            vmem((CHUNKS, NY, per, size), half),
            vmem((CHUNKS, NY - 1, per, size), half),
            vmem((CHUNKS, per, size), f32),
            vmem((CHUNKS, NY - 1, per, size), half),
            vmem((1, rows), f32),
            vmem((NY - 1, 1, rows), f32),
            vmem((1, rows), f32),
            vmem((1, rows), f32),
            vmem((1, rows), f32),
            vmem((rows, width), f32),
            vmem((2, width), f32),
            vmem((NR - 1, 2, width), f32),
            dma((3,)),
            dma((NZ - 1,)), dma((NZ,)), dma((NZ,)), dma((NZ,)),
            dma((NZ,)), dma((NZ,)), dma((NZ,)), dma((NZ,)),
            dma((CHUNKS, NY - 1)), dma((CHUNKS, NY - 1)), dma((CHUNKS,)), dma((CHUNKS,)),
            dma((CHUNKS,)), dma((CHUNKS,)), dma((CHUNKS, NY - 1)), dma((CHUNKS, NY - 1)),
            dma((NY,)), dma((NY,)), dma((NR - 1,)), dma((NR - 1,)),
        ],
        compiler_params=pltpu.CompilerParams(
            collective_id=0, has_side_effects=True, vmem_limit_bytes=60 * 2**20),
        cost_estimate=pl.CostEstimate(
            flops=2 * rows * NR * QB * cols, bytes_accessed=2 * rows * (cols + width), transcendentals=0),
        name="scores",
    )(gradients, queries, loss_weight.reshape(1, rows))


def solution(mesh):
    in_specs = (P("rows", "feat"), P("rows", "feat"), P("rows"))
    out_specs = P("rows", "feat")
    return jax.shard_map(body, mesh=mesh, in_specs=in_specs, out_specs=out_specs, check_vma=False)
```

time: 77.7 us -> 69.2 us (0.89)
  Pallas kernels: 73.7 us -> 67.4 us
  local copies, waits for them, and re-layouts: 3.74 us -> 1.67 us
    pallas_call x1, Pallas kernels: 73.7 us -> 67.4 us  [body(): pl.pallas_call(kernel, out_shape=jax.ShapeDtypeStruct((rows, width), jnp....]
    unnamed x7 -> x1, local copies, waits for them, and re-layouts: 3.74 us -> 1.67 us
where the time goes in v2:
time: 69.2 us; the launch traced here: 69.1 us
  Pallas kernels  67.4 us (97%)
  local copies, waits for them, and re-layouts  1.67 us (2%)
    pallas_call x1, Pallas kernels, body(): pl.pallas_call(kernel, out_shape=jax.ShapeDtypeStruct((rows, width), jnp....  67.4 us
    unnamed x1, local copies, waits for them, and re-layouts  1.67 us

profile of v2, /device:TPU:1, one launch (start us, length us, event | category | flops | bytes accessed | tf_op | source)
XLA Modules:
  0.0 69.1 jit_solution(5919693550476840728)
XLA Ops:
  0.0 67.4 %scores.1 = bf16[1024,128]{1,0:T(8,128)(2,1)} custom-call(bf16[1024,1024]{1,0:T(8,128)(2,1)} %g_hbm.1, bf16[16,1024]{1,0:T(8,128)(2,1)} %q_hbm.1, f32[1,1024]{1,0:T(1,128)} %bitcast.1), custom_call_target="tpu_custom_call" | custom-call | flops 2147483648 | bytes 2359296 | tf_op jit(solution)/shard_map/scores/pallas_call | solution.py:277
  67.4 1.7 %copy.5 = bf16[1024,128]{1,0:T(8,128)(2,1)} copy(bf16[1024,128]{1,0:T(8,128)(2,1)} %scores.1) | data formatting | bytes 524288

commit v3 on v2

v3 whole, which is shorter than its diff:
```python
import math
import jax
import jax.numpy as jnp
from jax import lax
from jax.experimental import pallas as pl
from jax.experimental.pallas import tpu as pltpu
from jax.sharding import PartitionSpec as P

NORM_EPS = 1e-06
VAR_EPS = 1e-05

NZ, NR, NF, NY = 16, 64, 8, 4
QB = 16
CHUNKS = 8
LANES = 128
KINDS = "YYYYYxxx"
MESH = pl.DeviceIdType.MESH
EARLY = (0, 1)
SCHEDULE = [(3, 0), (2, 4), (3, 1), (2, 5), (3, 2), (2, 6), (3, 3), (2, 7), (3, 4), (3, 5), (3, 6), (3, 7)]
SCHEDULE += [(4, i) for i in range(CHUNKS)]


FIRST, SECOND = (3, -3, 1, -1), (6, -6)
THIRD, LAST = (4, -4, 2, -2), (7, -7, 5, -5, 8)


def kernel(
    g_hbm, q_hbm, lw_hbm, o_hbm,
    o_ref, g, qall, lw, part, y_got, y_out, own, x_out, x_got,
    sq_mine, sq_got, sq_pair, sq_far, factor, turned, scored, stat_mine, stat_got,
    l_sem, o_sem, z_recv, x_recv, c_recv, y_recv, p_recv, s_recv, t_recv,
):
    r, f = lax.axis_index("rows"), lax.axis_index("feat")
    z, xh, c = r // 4, lax.rem(r // 2, 2), lax.rem(r, 2)
    y, xl = f // 2, lax.rem(f, 2)
    rows, cols = g.shape
    size = rows // 2
    portion = qall.shape[0] // 4
    per = portion // NF

    def at(dz, xh_to, c_to):
        return (lax.rem(z + dz + NZ, NZ) * 4 + xh_to * 2 + c_to, f)

    def y_peer(k):
        return (r, lax.rem(y + k, NY) * 2 + xl)

    x_peer = (r, y * 2 + 1 - xl)

    def block(dz, xh_of, c_of):
        first = (xh_of * 2 + c_of) * portion + lax.rem(z + dz + NZ, NZ) * QB
        return qall.at[pl.ds(pl.multiple_of(first, QB), QB)]

    def whole(xh_of, c_of):
        first = (xh_of * 2 + c_of) * portion
        return qall.at[pl.ds(pl.multiple_of(first, portion), portion)]

    loads = [
        pltpu.make_async_copy(q_hbm, block(0, xh, c), l_sem.at[0]),
        pltpu.make_async_copy(g_hbm, g, l_sem.at[1]),
        pltpu.make_async_copy(lw_hbm, lw, l_sem.at[2]),
    ]
    for load in loads:
        load.start()

    barrier = pltpu.get_barrier_semaphore()
    greet = [at(d, xh, c) for d in (3, -3, 4 * c - 2, 1, -1)]
    greet += [at(0, 1 - xh, c), at(0, xh, 1 - c), x_peer]
    greet += [y_peer(k) for k in range(1, NY)]
    for device in greet:
        pl.semaphore_signal(barrier, inc=1, device_id=device, device_id_type=MESH)
    loads[0].wait()
    pl.semaphore_wait(barrier, len(greet))

    sent = [0, 0, 0]

    def push(src, dst, group, rsem, device):
        pltpu.make_async_remote_copy(
            src_ref=src, dst_ref=dst, send_sem=o_sem.at[group], recv_sem=rsem,
            device_id=device, device_id_type=MESH).start()
        if group < 3:
            sent[group] += math.prod(src.shape) // cols

    def waiter(ref, ssem, rsem):
        return pltpu.make_async_remote_copy(
            src_ref=ref, dst_ref=ref, send_sem=ssem, recv_sem=rsem,
            device_id=at(0, xh, 1 - c), device_id_type=MESH)

    def landed(dst, rsem):
        waiter(dst, o_sem.at[0], rsem).wait_recv()

    def z_push(d, step):
        here = block(-d, xh, c)
        push(here, here, 0, z_recv.at[(d + step) % NZ], at(step, xh, c))

    def share(d):
        here = block(-d, xh, c)
        push(here, here, 0, x_recv.at[d % NZ], at(0, 1 - xh, c))
        push(here, here, 0, c_recv.at[0], at(0, xh, 1 - c))

    def share_x(ds):
        for d in ds:
            here = block(-d, 1 - xh, c)
            landed(here, x_recv.at[d % NZ])
            push(here, here, 0, c_recv.at[1], at(0, xh, 1 - c))

    for step in (3, -3):
        z_push(0, step)
    share(0)

    loads[1].wait()
    for i in range(rows // LANES):
        sums = jnp.zeros((LANES, LANES), jnp.float32)
        for j in range(cols // LANES):
            v = g[i * LANES:(i + 1) * LANES, j * LANES:(j + 1) * LANES].astype(jnp.float32)
            sums = sums + v * v
        sq_mine[:, i * LANES:(i + 1) * LANES] = jnp.sum(jnp.transpose(sums), axis=0, keepdims=True)
    for k in range(1, NY):
        push(sq_mine, sq_got.at[k - 1], 3, s_recv.at[0], y_peer(k))

    for d in FIRST:
        landed(block(-d, xh, c), z_recv.at[d % NZ])
        if abs(d) == 3:
            z_push(d, d)
        if d == -3:
            for step in (1, -1):
                z_push(0, step)
            for near in (3, -3):
                for step in (1, -1):
                    z_push(near, step)
            share(3)
        if d != 3:
            share(d)
    share_x((0,))
    for d in SECOND:
        landed(block(-d, xh, c), z_recv.at[d % NZ])
        z_push(d, 1)
        z_push(d, -1)
        if d == -6:
            turn = 1 - 2 * c
            here = block(-6 * turn, xh, c)
            push(here, here, 0, z_recv.at[8], at(2 * turn, xh, c))
        share(d)
    share_x(FIRST[:2])
    for d in THIRD:
        landed(block(-d, xh, c), z_recv.at[d % NZ])
        share(d)

    total = sq_mine[...]
    landed(sq_got, s_recv.at[0])
    for k in range(1, NY):
        total = total + sq_got[k - 1]
    sq_pair[...] = total
    push(sq_pair, sq_far, 4, s_recv.at[1], x_peer)
    share_x(FIRST[2:])

    for d in LAST:
        landed(block(-d, xh, c), z_recv.at[d % NZ])
        share(d)
    def y_row(k):
        return lax.rem(y + k + NY, NY)

    def source(i):
        return (xh if i < 4 else 1 - xh), (c if i % 4 < 2 else 1 - c)

    def span(i):
        return slice(i % 2 * size, (i % 2 + 1) * size)

    def y_push(i, src, slot, wide, k):
        dst = y_got.at[i, slot] if wide else y_got.at[i, slot, 0]
        alone = slot == 1 and KINDS[i] in "YX"
        push(src, dst, 1, y_recv.at[i, int(alone)], y_peer(k % NY))

    def y_wait(i, alone=False):
        if alone:
            ref = y_got.at[i, 1]
        else:
            ref = y_got.at[i, 0:2] if KINDS[i] in "YX" else y_got.at[i]
        if KINDS[i] in "Xx":
            ref = ref.at[0] if alone else ref.at[:, 0]
        landed(ref, y_recv.at[i, int(alone)])

    def sign(i):
        return 1 if i % 2 == 0 else -1

    def wide_part(i, k):
        return part.at[i, pl.ds(y_row(k) * 2, 2)]

    def multiply(i):
        value = lax.dot_general(
            whole(*source(i))[...], g[span(i), :],
            (((1,), (1,)), ((), ())), preferred_element_type=jnp.float32)
        y_first = KINDS[i] in "Yy"
        for b in range(NF):
            part[i, b if y_first else b % 2 * NY + b // 2] = value[b * per:(b + 1) * per].astype(jnp.bfloat16)
        s = sign(i)
        if KINDS[i] == "Y":
            y_push(i, wide_part(i, 2), 1, True, s)
            y_push(i, wide_part(i, -s), 0, True, -s)
        elif KINDS[i] == "y":
            for k in (2, 1, 3):
                y_push(i, wide_part(i, k), k - 1, True, k)
        else:
            push(part.at[i, pl.ds((1 - xl) * NY, NY)], x_got.at[i], 2, p_recv.at[i], x_peer)

    def second(i):
        s = sign(i)
        if KINDS[i] == "Y":
            y_wait(i, True)
            both = wide_part(i, s)[...].astype(jnp.float32) + y_got[i, 1].astype(jnp.float32)
            y_out[i, 0:2] = both.astype(jnp.bfloat16)
            y_push(i, y_out.at[i, 0:2], 2, True, s)
        elif KINDS[i] in "Xx":
            landed(x_got.at[i], p_recv.at[i])
            for k in (2, 1, 3, 0):
                to = y_row(k)
                both = part[i, xl * NY + to].astype(jnp.float32) + x_got[i, to].astype(jnp.float32)
                if k == 0:
                    own[i] = both
                    continue
                y_out[i, k - 1] = both.astype(jnp.bfloat16)
                if KINDS[i] == "x":
                    y_push(i, y_out.at[i, k - 1], k - 1, False, k)
                elif k == 2:
                    y_push(i, y_out.at[i, 1], 1, False, s)
                elif k == -s % NY:
                    y_push(i, y_out.at[i, k - 1], 0, False, -s)

    def third(i):
        s = sign(i)
        if KINDS[i] in "Yy":
            near = part[i, y * 2 + xl].astype(jnp.float32)
            far = part[i, y * 2 + 1 - xl].astype(jnp.float32)
            y_wait(i)
            for slot in (0, 2) if KINDS[i] == "Y" else (0, 1, 2):
                near = near + y_got[i, slot, xl].astype(jnp.float32)
                far = far + y_got[i, slot, 1 - xl].astype(jnp.float32)
            own[i] = near
            x_out[i] = far.astype(jnp.bfloat16)
            push(x_out.at[i], x_got.at[i, 0], 2, p_recv.at[i], x_peer)
        elif KINDS[i] == "X":
            y_wait(i, True)
            mine = s % NY - 1
            both = y_out[i, mine].astype(jnp.float32) + y_got[i, 1, 0].astype(jnp.float32)
            y_out[i, 3] = both.astype(jnp.bfloat16)
            y_push(i, y_out.at[i, 3], 2, False, s)

    def finish(i):
        raw = own[i]
        if KINDS[i] in "Yy":
            landed(x_got.at[i, 0], p_recv.at[i])
            raw = raw + x_got[i, 0].astype(jnp.float32)
        else:
            y_wait(i)
            for slot in (0, 2) if KINDS[i] == "X" else (0, 1, 2):
                raw = raw + y_got[i, slot, 0].astype(jnp.float32)
        raw = raw * factor[:, span(i)]
        xh_of, c_of = source(i)
        for low in range(per // QB):
            first = low * (4 * QB) + (xh_of * 2 + c_of) * QB
            turned[pl.ds(pl.multiple_of(first, QB), QB), span(i)] = raw[low * QB:(low + 1) * QB]

    def turn(h):
        value = jnp.transpose(turned[:, h * size:(h + 1) * size])
        scored[h * size:(h + 1) * size, :] = value
        return jnp.sum(value, axis=0, keepdims=True)

    multiply(0)
    multiply(1)
    share_x(SECOND)
    landed(whole(xh, 1 - c), c_recv.at[0])
    multiply(2)
    multiply(3)
    share_x(THIRD)
    share_x(LAST)
    multiply(4)
    multiply(5)
    for i in EARLY:
        second(i)
    landed(whole(1 - xh, 1 - c), c_recv.at[1])
    multiply(6)
    multiply(7)
    landed(sq_far, s_recv.at[1])
    loads[2].wait()
    factor[...] = lw[...] / jnp.sqrt((sq_pair[...] + sq_far[...]) / (cols * NF) + NORM_EPS)
    for i in range(4):
        if i not in EARLY:
            second(i)
    for step, i in SCHEDULE:
        (second, third, finish)[step - 2](i)
    column_sum = turn(0) + turn(1)
    own_mean = column_sum / rows
    off = scored[...] - own_mean
    stat_mine[0:1, :] = own_mean
    stat_mine[1:2, :] = jnp.sum(off * off, axis=0, keepdims=True)

    for i in sorted(range(1, NR), key=lambda i: abs(i - NR // 2)):
        push(stat_mine, stat_got.at[i - 1], 5, t_recv, (lax.rem(r + i, NR), f))
    for group, count in enumerate(sent):
        waiter(qall.at[pl.ds(0, count)], o_sem.at[group], t_recv).wait_send()
    waiter(sq_got, o_sem.at[3], t_recv).wait_send()
    waiter(sq_far, o_sem.at[4], t_recv).wait_send()
    stat_wait = waiter(stat_got, o_sem.at[5], t_recv)
    stat_wait.wait_recv()

    means = stat_got[:, 0, :]
    mean = (jnp.sum(means, axis=0, keepdims=True) + own_mean) / NR
    apart = means - mean
    own_apart = own_mean - mean
    spread = jnp.sum(stat_got[:, 1, :], axis=0, keepdims=True) + stat_mine[1:2, :]
    spread = spread + rows * (jnp.sum(apart * apart, axis=0, keepdims=True) + own_apart * own_apart)
    scale = lax.rsqrt(spread / (rows * NR) + VAR_EPS)
    o_ref[...] = ((scored[...] - mean) * scale).astype(o_ref.dtype)
    final = pltpu.make_async_copy(o_ref, o_hbm, l_sem.at[3])
    final.start()
    stat_wait.wait_send()
    final.wait()


def body(gradients, queries, loss_weight):
    rows, cols = gradients.shape
    width = queries.shape[0] * NR // NF
    per, size = width // 4, rows // 2
    half, f32 = jnp.bfloat16, jnp.float32
    vmem, dma = pltpu.VMEM, pltpu.SemaphoreType.DMA
    return pl.pallas_call(
        kernel,
        out_shape=jax.ShapeDtypeStruct((rows, width), jnp.bfloat16),
        in_specs=[pl.BlockSpec(memory_space=pltpu.HBM)] * 3,
        out_specs=pl.BlockSpec(memory_space=pltpu.HBM),
        scratch_shapes=[
            vmem((rows, width), half),
            vmem((rows, cols), half),
            vmem((NR * QB, cols), half),
            vmem((1, rows), f32),
            vmem((CHUNKS, NF, per, size), half),
            vmem((CHUNKS, NY - 1, 2, per, size), half),
            vmem((CHUNKS, NY, per, size), half),
            vmem((CHUNKS, per, size), f32),
            vmem((CHUNKS, per, size), half),
            vmem((CHUNKS, NY, per, size), half),
            vmem((1, rows), f32),
            vmem((NY - 1, 1, rows), f32),
            vmem((1, rows), f32),
            vmem((1, rows), f32),
            vmem((1, rows), f32),
            vmem((width, rows), f32),
            vmem((rows, width), f32),
            vmem((2, width), f32),
            vmem((NR - 1, 2, width), f32),
            dma((4,)), dma((6,)), dma((NZ,)), dma((NZ,)), dma((2,)),
            dma((CHUNKS, 2)), dma((CHUNKS,)), dma((2,)), dma,
        ],
        compiler_params=pltpu.CompilerParams(
            collective_id=0, has_side_effects=True, vmem_limit_bytes=60 * 2**20),
        cost_estimate=pl.CostEstimate(
            flops=2 * rows * NR * QB * cols, bytes_accessed=2 * rows * (cols + width), transcendentals=0),
        name="scores",
    )(gradients, queries, loss_weight.reshape(1, rows))


def solution(mesh):
    in_specs = (P("rows", "feat"), P("rows", "feat"), P("rows"))
    out_specs = P("rows", "feat")
    return jax.shard_map(body, mesh=mesh, in_specs=in_specs, out_specs=out_specs, check_vma=False)
```

time: 69.2 us -> 61.6 us (0.89)
  Pallas kernels: 67.4 us -> 59.8 us
    pallas_call x1, Pallas kernels: 67.4 us -> 59.8 us  [body(): pl.pallas_call(kernel, out_shape=jax.ShapeDtypeStruct((rows, width), jnp....]
where the time goes in v3:
time: 61.6 us; the launch traced here: 61.5 us
  Pallas kernels  59.8 us (97%)
  local copies, waits for them, and re-layouts  1.67 us (3%)
    pallas_call x1, Pallas kernels, body(): pl.pallas_call(kernel, out_shape=jax.ShapeDtypeStruct((rows, width), jnp....  59.8 us
    unnamed x1, local copies, waits for them, and re-layouts  1.67 us

profile of v3, /device:TPU:1, one launch (start us, length us, event | category | flops | bytes accessed | tf_op | source)
XLA Modules:
  0.0 61.5 jit_solution(700715994814137870)
XLA Ops:
  0.0 59.8 %scores.1 = bf16[1024,128]{1,0:T(8,128)(2,1)} custom-call(bf16[1024,1024]{1,0:T(8,128)(2,1)} %g_hbm.1, bf16[16,1024]{1,0:T(8,128)(2,1)} %q_hbm.1, f32[1,1024]{1,0:T(1,128)} %bitcast.1), custom_call_target="tpu_custom_call" | custom-call | flops 2147483648 | bytes 2359296 | tf_op jit(solution)/shard_map/scores/pallas_call | solution.py:325
  59.8 1.7 %copy.5 = bf16[1024,128]{1,0:T(8,128)(2,1)} copy(bf16[1024,128]{1,0:T(8,128)(2,1)} %scores.1) | data formatting | bytes 524288

commit v4 on v3

--- a/solution.py
+++ b/solution.py
@@ -25,8 +25,8 @@
 
 
 def kernel(
-    g_hbm, q_hbm, lw_hbm, o_hbm,
-    o_ref, g, qall, lw, part, y_got, y_out, own, x_out, x_got,
+    g_hbm, q_hbm, lw_hbm, o_ref,
+    g, qall, lw, part, y_got, y_out, own, x_out, x_got,
     sq_mine, sq_got, sq_pair, sq_far, factor, turned, scored, stat_mine, stat_got,
     l_sem, o_sem, z_recv, x_recv, c_recv, y_recv, p_recv, s_recv, t_recv,
 ):
@@ -103,7 +103,7 @@
             landed(here, x_recv.at[d % NZ])
             push(here, here, 0, c_recv.at[1], at(0, xh, 1 - c))
 
-    for step in (3, -3):
+    for step in (3, -3, 1, -1):
         z_push(0, step)
     share(0)
 
@@ -121,15 +121,11 @@
         landed(block(-d, xh, c), z_recv.at[d % NZ])
         if abs(d) == 3:
             z_push(d, d)
-        if d == -3:
-            for step in (1, -1):
-                z_push(0, step)
-            for near in (3, -3):
-                for step in (1, -1):
-                    z_push(near, step)
-            share(3)
-        if d != 3:
-            share(d)
+            if d == -3:
+                for near in (3, -3):
+                    for step in (1, -1):
+                        z_push(near, step)
+        share(d)
     share_x((0,))
     for d in SECOND:
         landed(block(-d, xh, c), z_recv.at[d % NZ])
@@ -310,10 +306,7 @@
     spread = spread + rows * (jnp.sum(apart * apart, axis=0, keepdims=True) + own_apart * own_apart)
     scale = lax.rsqrt(spread / (rows * NR) + VAR_EPS)
     o_ref[...] = ((scored[...] - mean) * scale).astype(o_ref.dtype)
-    final = pltpu.make_async_copy(o_ref, o_hbm, l_sem.at[3])
-    final.start()
     stat_wait.wait_send()
-    final.wait()
 
 
 def body(gradients, queries, loss_weight):
@@ -326,9 +319,8 @@
         kernel,
         out_shape=jax.ShapeDtypeStruct((rows, width), jnp.bfloat16),
         in_specs=[pl.BlockSpec(memory_space=pltpu.HBM)] * 3,
-        out_specs=pl.BlockSpec(memory_space=pltpu.HBM),
+        out_specs=pl.BlockSpec(memory_space=pltpu.VMEM),
         scratch_shapes=[
-            vmem((rows, width), half),
             vmem((rows, cols), half),
             vmem((NR * QB, cols), half),
             vmem((1, rows), f32),
@@ -347,15 +339,15 @@
             vmem((rows, width), f32),
             vmem((2, width), f32),
             vmem((NR - 1, 2, width), f32),
-            dma((4,)), dma((6,)), dma((NZ,)), dma((NZ,)), dma((2,)),
+            dma((3,)), dma((6,)), dma((NZ,)), dma((NZ,)), dma((2,)),
             dma((CHUNKS, 2)), dma((CHUNKS,)), dma((2,)), dma,
         ],
         compiler_params=pltpu.CompilerParams(
-            collective_id=0, has_side_effects=True, vmem_limit_bytes=60 * 2**20),
+            collective_id=0, has_side_effects=True, vmem_limit_bytes=48 * 2**20),
         cost_estimate=pl.CostEstimate(
             flops=2 * rows * NR * QB * cols, bytes_accessed=2 * rows * (cols + width), transcendentals=0),
         name="scores",
-    )(gradients, queries, loss_weight.reshape(1, rows))
+    )(*(pltpu.with_memory_space_constraint(v, pltpu.HBM) for v in (gradients, queries, loss_weight.reshape(1, rows))))
 
 
 def solution(mesh):

time: 61.6 us -> 59.8 us (0.971)
  local copies, waits for them, and re-layouts: 1.67 us -> 0.71 us
  Pallas kernels: 59.8 us -> 58.9 us
    unnamed x1, local copies, waits for them, and re-layouts: 1.67 us -> 0.71 us
    pallas_call x1, Pallas kernels: 59.8 us -> 58.9 us  [body(): pl.pallas_call(kernel, out_shape=jax.ShapeDtypeStruct((rows, width), jnp....]
where the time goes in v4:
time: 59.8 us; the launch traced here: 59.6 us
  Pallas kernels  58.9 us (98%)
  local copies, waits for them, and re-layouts  0.71 us (1%)
    pallas_call x1, Pallas kernels, body(): pl.pallas_call(kernel, out_shape=jax.ShapeDtypeStruct((rows, width), jnp....  58.9 us

profile of v4, /device:TPU:1, one launch (start us, length us, event | category | flops | bytes accessed | tf_op | source)
XLA Modules:
  0.0 59.6 jit_solution(13203037409150944871)
XLA Ops:
  0.0 58.9 %scores.1 = bf16[1024,128]{1,0:T(8,128)(2,1)S(1)} custom-call(bf16[1024,1024]{1,0:T(8,128)(2,1)} %g_hbm.1, bf16[16,1024]{1,0:T(8,128)(2,1)} %q_hbm.1, f32[1,1024]{1,0:T(1,128)} %bitcast.1), custom_call_target="tpu_custom_call" | custom-call | flops 2147483648 | bytes 2359296 | tf_op jit(solution)/shard_map/scores/pallas_call | solution.py:318
  58.9 0.7 %copy.5 = bf16[1024,128]{1,0:T(8,128)(2,1)} copy(bf16[1024,128]{1,0:T(8,128)(2,1)S(1)} %scores.1) | data formatting | bytes 524288

commit v5 on v4

--- a/solution.py
+++ b/solution.py
@@ -268,8 +268,8 @@
     multiply(3)
     share_x(THIRD)
     share_x(LAST)
+    multiply(5)
     multiply(4)
-    multiply(5)
     for i in EARLY:
         second(i)
     landed(whole(1 - xh, 1 - c), c_recv.at[1])

time: 59.8 us -> 58.9 us (0.985)
  Pallas kernels: 58.9 us -> 58.1 us
    pallas_call x1, Pallas kernels: 58.9 us -> 58.1 us  [body(): pl.pallas_call(kernel, out_shape=jax.ShapeDtypeStruct((rows, width), jnp....]
where the time goes in v5:
time: 58.9 us; the launch traced here: 58.8 us
  Pallas kernels  58.1 us (99%)
  local copies, waits for them, and re-layouts  0.71 us (1%)
    pallas_call x1, Pallas kernels, body(): pl.pallas_call(kernel, out_shape=jax.ShapeDtypeStruct((rows, width), jnp....  58.1 us

profile of v5, /device:TPU:1, one launch (start us, length us, event | category | flops | bytes accessed | tf_op | source)
XLA Modules:
  0.0 58.8 jit_solution(13347695853672774766)
XLA Ops:
  0.0 58.1 %scores.1 = bf16[1024,128]{1,0:T(8,128)(2,1)S(1)} custom-call(bf16[1024,1024]{1,0:T(8,128)(2,1)} %g_hbm.1, bf16[16,1024]{1,0:T(8,128)(2,1)} %q_hbm.1, f32[1,1024]{1,0:T(1,128)} %bitcast.1), custom_call_target="tpu_custom_call" | custom-call | flops 2147483648 | bytes 2359296 | tf_op jit(solution)/shard_map/scores/pallas_call | solution.py:318
  58.1 0.7 %copy.5 = bf16[1024,128]{1,0:T(8,128)(2,1)} copy(bf16[1024,128]{1,0:T(8,128)(2,1)S(1)} %scores.1) | data formatting | bytes 524288

commit v6 on v5

--- a/solution.py
+++ b/solution.py
@@ -13,7 +13,7 @@
 QB = 16
 CHUNKS = 8
 LANES = 128
-KINDS = "YYYYYxxx"
+KINDS = "YYYYyxxx"
 MESH = pl.DeviceIdType.MESH
 EARLY = (0, 1)
 SCHEDULE = [(3, 0), (2, 4), (3, 1), (2, 5), (3, 2), (2, 6), (3, 3), (2, 7), (3, 4), (3, 5), (3, 6), (3, 7)]

time: 58.9 us -> 58.9 us (level)
  no operation moved by 1% of the time
where the time goes in v6:
time: 58.9 us; the launch traced here: 58.8 us
  Pallas kernels  58.1 us (99%)
  local copies, waits for them, and re-layouts  0.71 us (1%)
    pallas_call x1, Pallas kernels, body(): pl.pallas_call(kernel, out_shape=jax.ShapeDtypeStruct((rows, width), jnp....  58.1 us

profile of v6, /device:TPU:1, one launch (start us, length us, event | category | flops | bytes accessed | tf_op | source)
XLA Modules:
  0.0 58.8 jit_solution(11859239339244433772)
XLA Ops:
  0.0 58.1 %scores.1 = bf16[1024,128]{1,0:T(8,128)(2,1)S(1)} custom-call(bf16[1024,1024]{1,0:T(8,128)(2,1)} %g_hbm.1, bf16[16,1024]{1,0:T(8,128)(2,1)} %q_hbm.1, f32[1,1024]{1,0:T(1,128)} %bitcast.1), custom_call_target="tpu_custom_call" | custom-call | flops 2147483648 | bytes 2359296 | tf_op jit(solution)/shard_map/scores/pallas_call | solution.py:318
  58.1 0.7 %copy.5 = bf16[1024,128]{1,0:T(8,128)(2,1)} copy(bf16[1024,128]{1,0:T(8,128)(2,1)S(1)} %scores.1) | data formatting | bytes 524288
